TPU v7x, 768 devices: a whole 4x8x12 slice. The times are simulated.
768 devices in a mesh: row: 12 (over z), col: 64 (over y, x, core).
Axes of the slice: x: 4, y: 8, z: 12, core: 2. Of those that a mesh axis runs over, the one named last changes fastest.
Arguments:
- features_t: bfloat16 [128, 393216], P('col', 'row'), may hold values from -6 to 6
- adjacency: int32 [12, 128, 128, 128], P('row'), may hold values from 0 to 3
- tile_dst: int32 [12, 128], P('row'), may hold values from 0 to 255
- tile_peer: int32 [12, 128], P('row'), may hold values from 0 to 11
- tile_slot: int32 [12, 128], P('row'), may hold values from 0 to 7, as said below
- offers: int32 [12, 12, 8], P('row'), may hold values from 0 to 255, as said below
- labels: int32 [393216], P(('row', 'col')), may hold values from 0 to 171
- w_self: bfloat16 [128, 256], replicated, may hold values from -0.5 to 0.5
- w_neigh: bfloat16 [128, 256], replicated, may hold values from -0.5 to 0.5
- w_class: bfloat16 [256, 172], replicated, may hold values from -0.375 to 0.375
Outputs:
- grad_features: bfloat16 [128, 393216], P('col', 'row')
- grad_self: float32 [128, 256], P('col')
- grad_neigh: float32 [128, 256], P('col')
- grad_class: float32 [256, 172], P('col')
Inputs may be any that keep to these rules, and one draw needn't show every extreme that they name: `tile_slot`: some tile of every row index reads slot 7. `offers`: the 8 block ids that one row index provides to one requester are distinct.
All inputs are finite; a program needn't handle non-finite values.
Results may differ from a plain program's by a relative error of at most 0.014.
Values may be sent and summed in bfloat16 or wider, within the bound.
A program may use at most 32 MiB of HBM per device.

v0:
```python
import jax
import jax.numpy as jnp
from jax import lax
from jax.sharding import PartitionSpec as P


def body(
    features_t, adjacency, tile_dst, tile_peer, tile_slot, offers, labels, w_self, w_neigh, w_class
):
    highest = lax.Precision.HIGHEST
    row_count = lax.axis_size("row")
    col_count = lax.axis_size("col")
    feat_cols, node_rows = features_t.shape
    block_size = adjacency.shape[2]
    block_count = node_rows // block_size
    slot_count = offers.shape[2]
    rows_here = labels.shape[0]
    class_count = w_class.shape[1]
    tile_weights = adjacency[0].astype(jnp.bfloat16)
    dest_block = tile_dst[0]
    source_slot = tile_peer[0] * slot_count + tile_slot[0]
    dest_onehot = (dest_block[:, None] == jnp.arange(block_count, dtype=jnp.int32)[None, :]).astype(
        jnp.float32
    )
    row_sums = jnp.sum(adjacency[0], axis=2).astype(jnp.float32)
    degree = jnp.dot(dest_onehot.T, row_sums, precision=highest)
    divisor = jnp.maximum(degree, 1.0)
    feature_blocks = features_t.reshape(feat_cols, block_count, block_size)
    outgoing = jnp.take(feature_blocks, offers[0], axis=1)
    incoming = lax.all_to_all(outgoing, "row", split_axis=1, concat_axis=1, tiled=True)
    sources = jnp.take(
        incoming.reshape(feat_cols, row_count * slot_count, block_size), source_slot, axis=1
    )
    products = jnp.einsum("ftj,tij->fti", sources, tile_weights, preferred_element_type=jnp.float32)
    summed = jnp.einsum("fti,tb->fbi", products, dest_onehot, precision=highest)
    aggregate = (summed / divisor[None]).astype(jnp.bfloat16).reshape(feat_cols, node_rows)
    rows_feat, rows_agg = (
        lax.all_to_all(features_t, "col", split_axis=1, concat_axis=0, tiled=True),
        lax.all_to_all(aggregate, "col", split_axis=1, concat_axis=0, tiled=True),
    )
    contract_first = (((0,), (0,)), ((), ()))
    contract_last = (((1,), (1,)), ((), ()))
    contract_inner = (((1,), (0,)), ((), ()))
    pre_act = lax.dot_general(
        rows_feat, w_self, contract_first, preferred_element_type=jnp.float32
    ) + lax.dot_general(rows_agg, w_neigh, contract_first, preferred_element_type=jnp.float32)
    sigmoid_act = jax.nn.sigmoid(pre_act)
    hidden = (pre_act * sigmoid_act).astype(jnp.bfloat16)
    logits = jnp.dot(hidden, w_class, preferred_element_type=jnp.float32)
    exponent = jnp.exp(logits)
    softmax_rows = exponent / jnp.sum(exponent, axis=1, keepdims=True)
    target = (labels[:, None] == jnp.arange(class_count, dtype=jnp.int32)[None, :]).astype(
        jnp.float32
    )
    dlogits = (softmax_rows - target).astype(jnp.bfloat16)
    back_hidden = lax.dot_general(
        dlogits, w_class, contract_last, preferred_element_type=jnp.float32
    )
    slope = sigmoid_act * (1.0 + pre_act * (1.0 - sigmoid_act))
    dpre = (back_hidden * slope).astype(jnp.bfloat16)
    node_total = rows_here * row_count * col_count
    factor = node_total ** (-0.5)
    self_part = (
        lax.dot_general(rows_feat, dpre, contract_inner, preferred_element_type=jnp.float32)
        * factor
    )
    neigh_part = (
        lax.dot_general(rows_agg, dpre, contract_inner, preferred_element_type=jnp.float32) * factor
    )
    class_part = (
        lax.dot_general(hidden, dlogits, contract_first, preferred_element_type=jnp.float32)
        * factor
    )
    self_back = lax.dot_general(
        w_self, dpre, contract_last, preferred_element_type=jnp.float32
    ).astype(jnp.bfloat16)
    my_divisor = lax.dynamic_slice_in_dim(
        divisor.reshape(node_rows), lax.axis_index("col") * rows_here, rows_here, 0
    )
    neigh_back = (
        lax.dot_general(w_neigh, dpre, contract_last, preferred_element_type=jnp.float32)
        / my_divisor[None, :]
    ).astype(jnp.bfloat16)
    cols_self, cols_neigh = (
        lax.all_to_all(self_back, "col", split_axis=0, concat_axis=1, tiled=True),
        lax.all_to_all(neigh_back, "col", split_axis=0, concat_axis=1, tiled=True),
    )
    dest_rows = jnp.take(cols_neigh.reshape(feat_cols, block_count, block_size), dest_block, axis=1)
    pushed = jnp.einsum("fti,tij->ftj", dest_rows, tile_weights, preferred_element_type=jnp.float32)
    slot_onehot = (
        source_slot[:, None] == jnp.arange(row_count * slot_count, dtype=jnp.int32)[None, :]
    ).astype(jnp.float32)
    per_slot = jnp.einsum("ftj,ts->fsj", pushed, slot_onehot, precision=highest).reshape(
        feat_cols, row_count, slot_count, block_size
    )
    returned = lax.all_to_all(per_slot, "row", split_axis=1, concat_axis=1, tiled=True)
    offer_onehot = (
        offers[0].reshape(row_count * slot_count)[:, None]
        == jnp.arange(block_count, dtype=jnp.int32)[None, :]
    ).astype(jnp.float32)
    landed = jnp.einsum(
        "fsj,sb->fbj",
        returned.reshape(feat_cols, row_count * slot_count, block_size),
        offer_onehot,
        precision=highest,
    ).reshape(feat_cols, node_rows)
    grad_features = (cols_self.astype(jnp.float32) + landed).astype(jnp.bfloat16)
    hidden_cols = w_class.shape[0] // col_count
    total_self, total_neigh, total_class = lax.psum(
        (self_part, neigh_part, class_part), ("row", "col")
    )
    position = lax.axis_index("col")
    grad_self = lax.dynamic_slice_in_dim(total_self, position * feat_cols, feat_cols, 0)
    grad_neigh = lax.dynamic_slice_in_dim(total_neigh, position * feat_cols, feat_cols, 0)
    grad_class = lax.dynamic_slice_in_dim(total_class, position * hidden_cols, hidden_cols, 0)
    return (grad_features, grad_self, grad_neigh, grad_class)


def solution(mesh):
    in_specs = (
        P("col", "row"),
        P("row", None, None, None),
        P("row", None),
        P("row", None),
        P("row", None),
        P("row", None, None),
        P(("row", "col")),
        P(),
        P(),
        P(),
    )
    out_specs = (P("col", "row"), P("col", None), P("col", None), P("col", None))
    return jax.shard_map(body, mesh=mesh, in_specs=in_specs, out_specs=out_specs, check_vma=False)
```

profile of v0, /device:TPU:1, one launch (start us, length us, event | category | flops | bytes accessed | tf_op | source)
XLA Modules:
  0.0 579.5 jit_solution(17162283603965254589)
XLA Ops:
  7.2 0.7 compare_and_fusion
  7.9 0.7 compare_select_fusion
  8.6 0.1 copy.29
  8.9 1.6 gather_fusion
  10.5 0.8 fusion.33
  11.3 15.7 %all-to-all-start.1 = ((bf16[2,12,8,128]{3,0,2,1:T(2,128)(2,1)}), bf16[2,12,8,128]{3,0,2,1:T(2,128)(2,1)S(1)}, u32[]{:S(2)}, u32[]{:S(2)}) async-start(bf16[2,12,8,128]{3,0,2,1:T(2,128)(2,1)} %fusion.33), calls=%async_computation.1 | async-start | bytes 98304 | tf_op jit(solution)/shard_map/all_to_all | solution.py:30
  27.0 0.7 fusion.40
  27.7 0.7 compare_and_fusion.2
  28.4 0.7 fusion.44
  29.0 0.7 compare_and_fusion.1
  29.7 5.7 reduce_sum.18
  35.4 0.2 convolution_maximum_fusion
  35.7 1.0 all-to-all-done.1
  36.7 12.2 %all-to-all-start = ((bf16[2,64,512]{2,0,1:T(2,128)(2,1)}), bf16[2,64,512]{2,0,1:T(2,128)(2,1)S(1)}, u32[]{:S(2)}, u32[]{:S(2)}) async-start(bf16[2,64,512]{2,0,1:T(2,128)(2,1)} %bitcast), calls=%async_computation | async-start | bytes 262144 | tf_op jit(solution)/shard_map/all_to_all | solution.py:38
  48.9 0.7 gather_fusion.1
  49.7 5.7 fusion.11
  55.3 0.3 fusion.10
  55.7 0.8 copy.32
  56.5 3.5 all-to-all-done
  60.0 6.8 %all-to-all-start.2 = ((bf16[2,64,512]{2,0,1:T(2,128)(2,1)}), bf16[2,64,512]{2,0,1:T(2,128)(2,1)S(1)}, u32[]{:S(2)}, u32[]{:S(2)}) async-start(bf16[2,64,512]{2,0,1:T(2,128)(2,1)} %copy.32), calls=%async_computation.2 | async-start | bytes 262144 | tf_op jit(solution)/shard_map/all_to_all | solution.py:39
  67.2 0.2 fusion.46
  67.4 10.5 %all-to-all-done.2 = bf16[2,64,512]{2,0,1:T(2,128)(2,1)S(1)} async-done(((bf16[2,64,512]{2,0,1:T(2,128)(2,1)}), bf16[2,64,512]{2,0,1:T(2,128)(2,1)S(1)}, u32[]{:S(2)}, u32[]{:S(2)}) %all-to-all-start.2) | async-done | bytes 131104 | tf_op jit(solution)/shard_map/all_to_all | solution.py:39
  78.0 0.2 convolution_add_fusion
  78.3 0.3 fusion.45
  78.6 0.3 fusion.6
  79.0 0.9 convolution_multiply_fusion.2
  79.8 0.9 fusion.17
  80.8 0.2 fusion.9
  81.0 0.7 all_to_all.67
  81.7 4.4 all-to-all-start.4
  86.2 0.2 fusion.18
  86.4 0.7 all_to_all.65
  87.1 1.1 convolution_multiply_fusion.1
  88.2 9.3 %all-to-all-done.4 = bf16[64,2,512]{2,1,0:T(2,128)(2,1)S(1)} async-done(((bf16[64,2,512]{2,1,0:T(2,128)(2,1)}), bf16[64,2,512]{2,1,0:T(2,128)(2,1)S(1)}, u32[]{:S(2)}, u32[]{:S(2)}) %all-to-all-start.4) | async-done | bytes 131104 | tf_op jit(solution)/shard_map/all_to_all | solution.py:86
  97.5 4.5 all-to-all-start.3
  101.9 0.7 gather_fusion.2
  102.7 4.6 fusion.14
  107.3 0.2 convolution_bitcast_fusion.1
  107.5 0.6 copy.38
  108.2 5.1 all-to-all-done.3
  113.3 7.2 %all-to-all-start.5 = ((f32[2,12,8,128]{3,2,0,1:T(8,128)}), f32[2,12,8,128]{3,2,0,1:T(8,128)S(1)}, u32[]{:S(2)}, u32[]{:S(2)}) async-start(f32[2,12,8,128]{3,2,0,1:T(8,128)} %copy.38), calls=%async_computation.5 | async-start | bytes 196608 | tf_op jit(solution)/shard_map/all_to_all | solution.py:96
  120.4 446.6 %all-reduce.3.cloned.1.call-done = (f32[128,256]{0,1:T(8,128)}, f32[128,256]{1,0:T(8,128)}, f32[256,172]{1,0:T(8,128)}) async-done(((f32[128,256]{0,1:T(8,128)}, f32[128,256]{1,0:T(8,128)}, f32[256,172]{1,0:T(8,128)}), (f32[128,256]{0,1:T(8,128)}, f32[128,256]{1,0:T(8,128)}, f32[256,172]{1,0:T(8,128)})) %all-reduce.3.cloned.1.call-update) | async-done | bytes 438288 | tf_op jit(solution)/shard_map/psum | solution.py:109
  567.0 1.0 constant_dynamic-slice_fusion.2
  568.0 0.7 copy.40
  568.7 1.3 constant_dynamic-slice_fusion.1
  569.9 1.3 constant_dynamic-slice_fusion
  571.3 0.4 convolution_bitcast_fusion
  571.7 0.9 fusion.19
  (28 shorter events, 0.8 us)
Async XLA Ops:
  7.2 71.1 %copy-start = (bf16[256,172]{0,1:T(8,128)(2,1)S(1)}, bf16[256,172]{0,1:T(8,128)(2,1)}, u32[]{:S(2)}) copy-start(bf16[256,172]{0,1:T(8,128)(2,1)} %param.19) | copy-start | bytes 264196
  7.2 28.2 %copy-start.4 = (s32[1,128]{1,0:T(1,128)S(1)}, s32[1,128]{1,0:T(1,128)}, u32[]{:S(2)}) copy-start(s32[1,128]{1,0:T(1,128)} %param.12) | copy-start | bytes 1540
  11.3 25.4 %all-to-all-start.1 = ((bf16[2,12,8,128]{3,0,2,1:T(2,128)(2,1)}), bf16[2,12,8,128]{3,0,2,1:T(2,128)(2,1)S(1)}, u32[]{:S(2)}, u32[]{:S(2)}) async-start(bf16[2,12,8,128]{3,0,2,1:T(2,128)(2,1)} %fusion.33), calls=%async_computation.1 | async-start | bytes 98304 | tf_op jit(solution)/shard_map/all_to_all | solution.py:30
  29.7 37.2 %copy-start.3 = (s32[1,12,8]{1,2,0:T(8,128)S(1)}, s32[1,12,8]{1,2,0:T(8,128)}, u32[]{:S(2)}) copy-start(s32[1,12,8]{1,2,0:T(8,128)} %param.15) | copy-start | bytes 1156
  29.7 37.5 %copy-start.1 = (bf16[128,256]{1,0:T(8,128)(2,1)S(1)}, bf16[128,256]{1,0:T(8,128)(2,1)}, u32[]{:S(2)}) copy-start(bf16[128,256]{1,0:T(8,128)(2,1)} %param.17) | copy-start | bytes 196612
  29.7 48.3 %copy-start.2 = (bf16[128,256]{1,0:T(8,128)(2,1)S(1)}, bf16[128,256]{1,0:T(8,128)(2,1)}, u32[]{:S(2)}) copy-start(bf16[128,256]{1,0:T(8,128)(2,1)} %param.18) | copy-start | bytes 196612
  35.4 43.2 %copy-start.5 = (s32[512]{0:T(512)S(1)}, s32[512]{0:T(512)}, u32[]{:S(2)}) copy-start(s32[512]{0:T(512)} %param.16) | copy-start | bytes 6148
  36.7 23.3 %all-to-all-start = ((bf16[2,64,512]{2,0,1:T(2,128)(2,1)}), bf16[2,64,512]{2,0,1:T(2,128)(2,1)S(1)}, u32[]{:S(2)}, u32[]{:S(2)}) async-start(bf16[2,64,512]{2,0,1:T(2,128)(2,1)} %bitcast), calls=%async_computation | async-start | bytes 262144 | tf_op jit(solution)/shard_map/all_to_all | solution.py:38
  60.0 17.9 %all-to-all-start.2 = ((bf16[2,64,512]{2,0,1:T(2,128)(2,1)}), bf16[2,64,512]{2,0,1:T(2,128)(2,1)S(1)}, u32[]{:S(2)}, u32[]{:S(2)}) async-start(bf16[2,64,512]{2,0,1:T(2,128)(2,1)} %copy.32), calls=%async_computation.2 | async-start | bytes 262144 | tf_op jit(solution)/shard_map/all_to_all | solution.py:39
  81.7 15.8 %all-to-all-start.4 = ((bf16[64,2,512]{2,1,0:T(2,128)(2,1)}), bf16[64,2,512]{2,1,0:T(2,128)(2,1)S(1)}, u32[]{:S(2)}, u32[]{:S(2)}) async-start(bf16[64,2,512]{2,1,0:T(2,128)(2,1)} %all_to_all.67), calls=%async_computation.4 | async-start | bytes 262144 | tf_op jit(solution)/shard_map/all_to_all | solution.py:86
  86.1 480.9 %all-reduce.3.cloned.1.call-start = ((), (), s32[]{:S(2)}) async-start(), calls=%async_computation.6 | async-start | bytes 1048576 | tf_op jit(solution)/shard_map/psum | solution.py:109
  97.5 15.8 %all-to-all-start.3 = ((bf16[64,2,512]{2,1,0:T(2,128)(2,1)}), bf16[64,2,512]{2,1,0:T(2,128)(2,1)S(1)}, u32[]{:S(2)}, u32[]{:S(2)}) async-start(bf16[64,2,512]{2,1,0:T(2,128)(2,1)} %all_to_all.65), calls=%async_computation.3 | async-start | bytes 262144 | tf_op jit(solution)/shard_map/all_to_all | solution.py:85
  113.3 458.1 %all-to-all-start.5 = ((f32[2,12,8,128]{3,2,0,1:T(8,128)}), f32[2,12,8,128]{3,2,0,1:T(8,128)S(1)}, u32[]{:S(2)}, u32[]{:S(2)}) async-start(f32[2,12,8,128]{3,2,0,1:T(8,128)} %copy.38), calls=%async_computation.5 | async-start | bytes 196608 | tf_op jit(solution)/shard_map/all_to_all | solution.py:96
Sparse Core Ops, SparseCore 0:
  93.0 473.9 all-reduce.2
where the time goes:
time: 580 us
  waiting for transfers between devices  476 us (82%)
  starting transfers between devices  50.8 us (9%)
  matrix products  15.9 us (3%)
  between operations  14.3 us (2%)
  other arithmetic  11.6 us (2%)
  local copies, waits for them, and re-layouts  10.9 us (2%)
    psum x1, waiting for transfers between devices, body(): lax.psum((self_part, neigh_part, class_part), ('row', 'col'))  447 us
    all_to_all x1, starting transfers between devices, body(): lax.all_to_all(outgoing, 'row', split_axis=1, concat_axis=1, tiled=True)  15.7 us
    all_to_all x1, starting transfers between devices, body(): lax.all_to_all(features_t, 'col', split_axis=1, concat_axis=0, tiled=True)  12.2 us
  transfers between devices with their start and end apart: 7, of which 6 were waited for; matrix products, arithmetic and copies ran while one was open for 5% of the time, Pallas kernels for 0%

commit v1 on v0

--- a/solution.py
+++ b/solution.py
@@ -1,7 +1,95 @@
 import jax
 import jax.numpy as jnp
 from jax import lax
+from jax.experimental import pallas as pl
+from jax.experimental.pallas import tpu as pltpu
 from jax.sharding import PartitionSpec as P
+
+MESH = pl.DeviceIdType.MESH
+
+
+def reduce_kernel(w_ref, out_ref, half, mine, got, rows, send, recv):
+    row_count = lax.axis_size("row")
+    chip_count = lax.axis_size("col") // 2
+    row, col = lax.axis_index("row"), lax.axis_index("col")
+    chip, core = col // 2, col % 2
+    sibling = (row, chip * 2 + 1 - core)
+
+    def chip_at(step):
+        other = lax.rem(chip + step, chip_count)
+        return other, (row, other * 2 + core)
+
+    def row_at(step):
+        return (lax.rem(row + step, row_count), col)
+
+    barrier = pltpu.get_barrier_semaphore()
+
+    def greet(device):
+        pl.semaphore_signal(barrier, inc=1, device_id=device, device_id_type=MESH)
+
+    greet(sibling)
+
+    @pl.loop(1, chip_count)
+    def _(step):
+        greet(chip_at(step)[1])
+
+    @pl.loop(1, row_count)
+    def _(step):
+        greet(row_at(step))
+
+    pl.semaphore_wait(barrier, chip_count + row_count - 1)
+    swap = pltpu.make_async_remote_copy(
+        w_ref.at[1 - core], half, send.at[0], recv.at[0], device_id=sibling, device_id_type=MESH
+    )
+    swap.start()
+    swap.wait()
+    mine[...] = w_ref[core] + half[...]
+    got[chip] = mine[chip]
+
+    @pl.loop(1, chip_count)
+    def _(step):
+        other, device = chip_at(step)
+        pltpu.make_async_remote_copy(
+            mine.at[other], got.at[chip], send.at[1], recv.at[1], device_id=device, device_id_type=MESH
+        ).start()
+
+    others = got.at[pl.ds(0, chip_count - 1)]
+    pltpu.make_async_copy(others, others, recv.at[1]).wait()
+    rows[row] = jnp.sum(got[...], axis=0)
+
+    @pl.loop(1, row_count)
+    def _(step):
+        pltpu.make_async_remote_copy(
+            rows.at[row], rows.at[row], send.at[2], recv.at[2], device_id=row_at(step), device_id_type=MESH
+        ).start()
+
+    others_row = rows.at[pl.ds(0, row_count - 1)]
+    pltpu.make_async_copy(others_row, others_row, recv.at[2]).wait()
+    out_ref[...] = jnp.sum(rows[...], axis=0)
+    pltpu.make_async_copy(others, others, send.at[1]).wait()
+    pltpu.make_async_copy(others_row, others_row, send.at[2]).wait()
+
+
+def reduce_weights(weights):
+    cores, chips, height, width = weights.shape
+    row_count = lax.axis_size("row")
+    return pl.pallas_call(
+        reduce_kernel,
+        out_shape=jax.ShapeDtypeStruct((height, width), jnp.float32),
+        in_specs=[pl.BlockSpec(memory_space=pltpu.VMEM)],
+        out_specs=pl.BlockSpec(memory_space=pltpu.VMEM),
+        scratch_shapes=[
+            pltpu.VMEM((chips, height, width), jnp.float32),
+            pltpu.VMEM((chips, height, width), jnp.float32),
+            pltpu.VMEM((chips, height, width), jnp.float32),
+            pltpu.VMEM((row_count, height, width), jnp.float32),
+            pltpu.SemaphoreType.DMA((3,)),
+            pltpu.SemaphoreType.DMA((3,)),
+        ],
+        compiler_params=pltpu.CompilerParams(
+            collective_id=0, has_side_effects=True, vmem_limit_bytes=16 << 20
+        ),
+    )(weights)
 
 
 def body(
@@ -106,13 +194,24 @@
     ).reshape(feat_cols, node_rows)
     grad_features = (cols_self.astype(jnp.float32) + landed).astype(jnp.bfloat16)
     hidden_cols = w_class.shape[0] // col_count
-    total_self, total_neigh, total_class = lax.psum(
-        (self_part, neigh_part, class_part), ("row", "col")
-    )
-    position = lax.axis_index("col")
-    grad_self = lax.dynamic_slice_in_dim(total_self, position * feat_cols, feat_cols, 0)
-    grad_neigh = lax.dynamic_slice_in_dim(total_neigh, position * feat_cols, feat_cols, 0)
-    grad_class = lax.dynamic_slice_in_dim(total_class, position * hidden_cols, hidden_cols, 0)
+    hidden_units = w_self.shape[1]
+    packed = jnp.concatenate(
+        [
+            self_part.reshape(col_count, feat_cols, hidden_units),
+            neigh_part.reshape(col_count, feat_cols, hidden_units),
+            jnp.pad(
+                class_part.reshape(col_count, hidden_cols, class_count),
+                ((0, 0), (0, 0), (0, hidden_units - class_count)),
+            ),
+        ],
+        axis=1,
+    )
+    total = reduce_weights(
+        packed.reshape(col_count // 2, 2, -1, hidden_units).transpose(1, 0, 2, 3)
+    )
+    grad_self = total[:feat_cols]
+    grad_neigh = total[feat_cols : 2 * feat_cols]
+    grad_class = total[2 * feat_cols :, :class_count]
     return (grad_features, grad_self, grad_neigh, grad_class)
 
 

time: 580 us -> 143 us (0.25)
  waiting for transfers between devices: 476 us -> 29.9 us
  Pallas kernels: 0 us -> 25.4 us
  between operations: 14.3 us -> 0.99 us
    psum x1 -> x0, waiting for transfers between devices: 447 us -> none  [body(): lax.psum((self_part, neigh_part, class_part), ('row', 'col'))]
    pallas_call x0 -> x1, Pallas kernels: none -> 25.4 us  [reduce_weights(): pl.pallas_call(reduce_kernel, out_shape=jax.ShapeDtypeStruct((height, wid...]
  transfers between devices with their start and end apart: 7 -> 6, of which waited for: 6 -> 5; matrix products, arithmetic and copies ran while one was open for 5% -> 18% of each run, Pallas kernels for 0% -> 18%
where the time goes in v1:
time: 143 us; the launch traced here: 141 us
  starting transfers between devices  50.8 us (36%)
  waiting for transfers between devices  29.9 us (21%)
  Pallas kernels  25.4 us (18%)
  matrix products  13.6 us (10%)
  other arithmetic  11.8 us (8%)
  local copies, waits for them, and re-layouts  8.26 us (6%)
    pallas_call x1, Pallas kernels, reduce_weights(): pl.pallas_call(reduce_kernel, out_shape=jax.ShapeDtypeStruct((height, wid...  25.4 us
    all_to_all x1, starting transfers between devices, body(): lax.all_to_all(outgoing, 'row', split_axis=1, concat_axis=1, tiled=True)  15.7 us
    all_to_all x1, starting transfers between devices, body(): lax.all_to_all(features_t, 'col', split_axis=1, concat_axis=0, tiled=True)  12.2 us
    all_to_all x1, waiting for transfers between devices, body(): lax.all_to_all(aggregate, 'col', split_axis=1, concat_axis=0, tiled=True)  10.5 us
    all_to_all x1, waiting for transfers between devices, body(): lax.all_to_all(neigh_back, 'col', split_axis=0, concat_axis=1, tiled=True)  9.78 us
    all_to_all x1, starting transfers between devices, body(): lax.all_to_all(per_slot, 'row', split_axis=1, concat_axis=1, tiled=True)  7.16 us
    all_to_all x1, starting transfers between devices, body(): lax.all_to_all(aggregate, 'col', split_axis=1, concat_axis=0, tiled=True)  6.79 us
    dot_general x1, matrix products, body(): jnp.einsum('ftj,tij->fti', sources, tile_weights, preferred_element_type=...  5.68 us
  transfers between devices with their start and end apart: 6, of which 5 were waited for; matrix products, arithmetic and copies ran while one was open for 18% of the time, Pallas kernels for 18%

profile of v1, /device:TPU:1, one launch (start us, length us, event | category | flops | bytes accessed | tf_op | source)
XLA Modules:
  0.0 140.8 jit_solution(10354301961755106764)
XLA Ops:
  0.7 0.7 compare_and_fusion
  1.4 0.7 compare_select_fusion
  2.1 0.1 copy.31
  2.4 1.6 %gather_fusion = bf16[96,2,128]{2,1,0:T(2,128)(2,1)S(1)} fusion(bf16[2,256,128]{2,0,1:T(2,128)(2,1)} %bitcast.6, s32[1024]{0:T(1024)S(1)} %pad_clamp_fusion.2), kind=kCustom, calls=%fused_computation | custom fusion | bytes 98688 | tf_op jit(solution)/shard_map/jit(_take)/gather | solution.py:117
  4.0 0.8 fusion.33
  4.8 15.7 %all-to-all-start.1 = ((bf16[2,12,8,128]{3,0,2,1:T(2,128)(2,1)}), bf16[2,12,8,128]{3,0,2,1:T(2,128)(2,1)S(1)}, u32[]{:S(2)}, u32[]{:S(2)}) async-start(bf16[2,12,8,128]{3,0,2,1:T(2,128)(2,1)} %fusion.33), calls=%async_computation.1 | async-start | bytes 98304 | tf_op jit(solution)/shard_map/all_to_all | solution.py:118
  20.5 0.7 fusion.40
  21.2 0.7 compare_and_fusion.2
  21.8 0.7 fusion.44
  22.5 0.7 compare_and_fusion.1
  23.2 5.7 %reduce_sum.18 = s32[128,128]{1,0:T(8,128)S(1)} reduce(s32[1,128,128,128]{3,2,1,0:T(8,128)} %param.11, s32[]{:T(128)} %constant.27.clone.1), dimensions={0,3}, to_apply=%region_0.0 | reduce | flops 2080768 | bytes 8454148 | tf_op jit(solution)/shard_map/reduce_sum | solution.py:113
  28.9 0.2 convolution_maximum_fusion
  29.1 1.0 all-to-all-done.1
  30.2 12.2 %all-to-all-start = ((bf16[2,64,512]{2,0,1:T(2,128)(2,1)}), bf16[2,64,512]{2,0,1:T(2,128)(2,1)S(1)}, u32[]{:S(2)}, u32[]{:S(2)}) async-start(bf16[2,64,512]{2,0,1:T(2,128)(2,1)} %bitcast), calls=%async_computation | async-start | bytes 262144 | tf_op jit(solution)/shard_map/all_to_all | solution.py:126
  42.4 0.7 gather_fusion.1
  43.1 5.7 %fusion.11 = f32[2,128,128]{2,0,1:T(2,128)S(1)} fusion(s32[1,128,128,128]{3,2,1,0:T(8,128)} %param.11, bf16[128,2,128]{2,1,0:T(2,128)(2,1)S(1)} %gather_fusion.1, pred[128]{0:T(512)(128)(4,1)S(1)} %compare_and_fusion.2), kind=kOutput, calls=%fused_computation.22 | convolution fusion | flops 10518528 | bytes 8585344 | tf_op jit(solution)/shard_map/ftj,tij->fti/dot_general | solution.py:122
  48.8 0.3 fusion.10
  49.2 0.8 copy.34
  50.0 3.5 %all-to-all-done = bf16[2,64,512]{2,0,1:T(2,128)(2,1)S(1)} async-done(((bf16[2,64,512]{2,0,1:T(2,128)(2,1)}), bf16[2,64,512]{2,0,1:T(2,128)(2,1)S(1)}, u32[]{:S(2)}, u32[]{:S(2)}) %all-to-all-start) | async-done | bytes 131104 | tf_op jit(solution)/shard_map/all_to_all | solution.py:126
  53.5 6.8 %all-to-all-start.2 = ((bf16[2,64,512]{2,0,1:T(2,128)(2,1)}), bf16[2,64,512]{2,0,1:T(2,128)(2,1)S(1)}, u32[]{:S(2)}, u32[]{:S(2)}) async-start(bf16[2,64,512]{2,0,1:T(2,128)(2,1)} %copy.34), calls=%async_computation.2 | async-start | bytes 262144 | tf_op jit(solution)/shard_map/all_to_all | solution.py:127
  60.6 0.2 fusion.47
  60.9 10.5 %all-to-all-done.2 = bf16[2,64,512]{2,0,1:T(2,128)(2,1)S(1)} async-done(((bf16[2,64,512]{2,0,1:T(2,128)(2,1)}), bf16[2,64,512]{2,0,1:T(2,128)(2,1)S(1)}, u32[]{:S(2)}, u32[]{:S(2)}) %all-to-all-start.2) | async-done | bytes 131104 | tf_op jit(solution)/shard_map/all_to_all | solution.py:127
  71.5 0.3 multiply_convert_fusion
  71.8 0.3 fusion.46
  72.1 0.2 convolution_multiply_fusion.1
  72.3 0.3 fusion.6
  72.7 0.2 convolution_multiply_fusion.3
  72.9 0.2 fusion.9
  73.1 0.7 all_to_all.67
  73.8 4.4 %all-to-all-start.4 = ((bf16[64,2,512]{2,1,0:T(2,128)(2,1)}), bf16[64,2,512]{2,1,0:T(2,128)(2,1)S(1)}, u32[]{:S(2)}, u32[]{:S(2)}) async-start(bf16[64,2,512]{2,1,0:T(2,128)(2,1)} %all_to_all.67), calls=%async_computation.4 | async-start | bytes 262144 | tf_op jit(solution)/shard_map/all_to_all | solution.py:174
  78.3 0.2 fusion.17
  78.6 0.1 copy.42
  78.8 0.2 fusion.18
  79.1 0.7 all_to_all.65
  79.8 9.8 %all-to-all-done.4 = bf16[64,2,512]{2,1,0:T(2,128)(2,1)S(1)} async-done(((bf16[64,2,512]{2,1,0:T(2,128)(2,1)}), bf16[64,2,512]{2,1,0:T(2,128)(2,1)S(1)}, u32[]{:S(2)}, u32[]{:S(2)}) %all-to-all-start.4) | async-done | bytes 131104 | tf_op jit(solution)/shard_map/all_to_all | solution.py:174
  89.6 4.5 %all-to-all-start.3 = ((bf16[64,2,512]{2,1,0:T(2,128)(2,1)}), bf16[64,2,512]{2,1,0:T(2,128)(2,1)S(1)}, u32[]{:S(2)}, u32[]{:S(2)}) async-start(bf16[64,2,512]{2,1,0:T(2,128)(2,1)} %all_to_all.65), calls=%async_computation.3 | async-start | bytes 262144 | tf_op jit(solution)/shard_map/all_to_all | solution.py:173
  94.1 0.7 gather_fusion.2
  94.8 4.6 %fusion.14 = f32[2,128,128]{2,0,1:T(2,128)S(1)} fusion(s32[1,128,128,128]{3,2,1,0:T(8,128)} %param.11, bf16[128,2,128]{2,1,0:T(2,128)(2,1)S(1)} %gather_fusion.2, pred[128]{0:T(512)(128)(4,1)S(1)} %compare_and_fusion.1), kind=kOutput, calls=%fused_computation.23 | convolution fusion | flops 10518528 | bytes 8585344 | tf_op jit(solution)/shard_map/fti,tij->ftj/dot_general | solution.py:177
  99.4 0.2 convolution_bitcast_fusion.1
  99.7 0.7 copy.40
  100.3 5.1 %all-to-all-done.3 = bf16[64,2,512]{2,1,0:T(2,128)(2,1)S(1)} async-done(((bf16[64,2,512]{2,1,0:T(2,128)(2,1)}), bf16[64,2,512]{2,1,0:T(2,128)(2,1)S(1)}, u32[]{:S(2)}, u32[]{:S(2)}) %all-to-all-start.3) | async-done | bytes 131104 | tf_op jit(solution)/shard_map/all_to_all | solution.py:173
  105.4 7.2 %all-to-all-start.5 = ((f32[2,12,8,128]{3,2,0,1:T(8,128)}), f32[2,12,8,128]{3,2,0,1:T(8,128)S(1)}, u32[]{:S(2)}, u32[]{:S(2)}) async-start(f32[2,12,8,128]{3,2,0,1:T(8,128)} %copy.40), calls=%async_computation.5 | async-start | bytes 196608 | tf_op jit(solution)/shard_map/all_to_all | solution.py:184
  112.6 0.2 copy_bitcast_fusion.w_ref
  112.8 25.4 %shard_map.129 = f32[8,256]{1,0:T(8,128)S(1)} custom-call(f32[2,32,8,256]{3,2,1,0:T(8,128)S(1)} %copy_bitcast_fusion.w_ref), custom_call_target="tpu_custom_call" | custom-call | tf_op jit(solution)/shard_map/pallas_call | solution.py:76
  138.2 0.6 slice.11
  138.8 0.6 fusion.45
  139.5 0.4 convolution_bitcast_fusion
  139.9 0.9 fusion.19
  (30 shorter events, 1.0 us)
Async XLA Ops:
  0.6 71.2 %copy-start = (bf16[256,172]{0,1:T(8,128)(2,1)S(1)}, bf16[256,172]{0,1:T(8,128)(2,1)}, u32[]{:S(2)}) copy-start(bf16[256,172]{0,1:T(8,128)(2,1)} %param.19) | copy-start | bytes 264196
  0.6 28.2 %copy-start.3 = (s32[1,128]{1,0:T(1,128)S(1)}, s32[1,128]{1,0:T(1,128)}, u32[]{:S(2)}) copy-start(s32[1,128]{1,0:T(1,128)} %param.12) | copy-start | bytes 1540
  4.8 25.4 %all-to-all-start.1 = ((bf16[2,12,8,128]{3,0,2,1:T(2,128)(2,1)}), bf16[2,12,8,128]{3,0,2,1:T(2,128)(2,1)S(1)}, u32[]{:S(2)}, u32[]{:S(2)}) async-start(bf16[2,12,8,128]{3,0,2,1:T(2,128)(2,1)} %fusion.33), calls=%async_computation.1 | async-start | bytes 98304 | tf_op jit(solution)/shard_map/all_to_all | solution.py:118
  23.2 37.1 %copy-start.2 = (s32[1,12,8]{1,2,0:T(8,128)S(1)}, s32[1,12,8]{1,2,0:T(8,128)}, u32[]{:S(2)}) copy-start(s32[1,12,8]{1,2,0:T(8,128)} %param.15) | copy-start | bytes 1156
  23.2 37.5 %copy-start.1 = (bf16[128,256]{1,0:T(8,128)(2,1)S(1)}, bf16[128,256]{1,0:T(8,128)(2,1)}, u32[]{:S(2)}) copy-start(bf16[128,256]{1,0:T(8,128)(2,1)} %param.17) | copy-start | bytes 196612
  23.2 48.3 %copy-start.4 = (bf16[128,256]{1,0:T(8,128)(2,1)S(1)}, bf16[128,256]{1,0:T(8,128)(2,1)}, u32[]{:S(2)}) copy-start(bf16[128,256]{1,0:T(8,128)(2,1)} %param.18) | copy-start | bytes 196612
  28.9 43.2 %copy-start.5 = (s32[512]{0:T(512)S(1)}, s32[512]{0:T(512)}, u32[]{:S(2)}) copy-start(s32[512]{0:T(512)} %param.16) | copy-start | bytes 6148
  30.2 23.3 %all-to-all-start = ((bf16[2,64,512]{2,0,1:T(2,128)(2,1)}), bf16[2,64,512]{2,0,1:T(2,128)(2,1)S(1)}, u32[]{:S(2)}, u32[]{:S(2)}) async-start(bf16[2,64,512]{2,0,1:T(2,128)(2,1)} %bitcast), calls=%async_computation | async-start | bytes 262144 | tf_op jit(solution)/shard_map/all_to_all | solution.py:126
  53.5 17.9 %all-to-all-start.2 = ((bf16[2,64,512]{2,0,1:T(2,128)(2,1)}), bf16[2,64,512]{2,0,1:T(2,128)(2,1)S(1)}, u32[]{:S(2)}, u32[]{:S(2)}) async-start(bf16[2,64,512]{2,0,1:T(2,128)(2,1)} %copy.34), calls=%async_computation.2 | async-start | bytes 262144 | tf_op jit(solution)/shard_map/all_to_all | solution.py:127
  73.8 15.8 %all-to-all-start.4 = ((bf16[64,2,512]{2,1,0:T(2,128)(2,1)}), bf16[64,2,512]{2,1,0:T(2,128)(2,1)S(1)}, u32[]{:S(2)}, u32[]{:S(2)}) async-start(bf16[64,2,512]{2,1,0:T(2,128)(2,1)} %all_to_all.67), calls=%async_computation.4 | async-start | bytes 262144 | tf_op jit(solution)/shard_map/all_to_all | solution.py:174
  89.6 15.8 %all-to-all-start.3 = ((bf16[64,2,512]{2,1,0:T(2,128)(2,1)}), bf16[64,2,512]{2,1,0:T(2,128)(2,1)S(1)}, u32[]{:S(2)}, u32[]{:S(2)}) async-start(bf16[64,2,512]{2,1,0:T(2,128)(2,1)} %all_to_all.65), calls=%async_computation.3 | async-start | bytes 262144 | tf_op jit(solution)/shard_map/all_to_all | solution.py:173
  105.4 34.1 %all-to-all-start.5 = ((f32[2,12,8,128]{3,2,0,1:T(8,128)}), f32[2,12,8,128]{3,2,0,1:T(8,128)S(1)}, u32[]{:S(2)}, u32[]{:S(2)}) async-start(f32[2,12,8,128]{3,2,0,1:T(8,128)} %copy.40), calls=%async_computation.5 | async-start | bytes 196608 | tf_op jit(solution)/shard_map/all_to_all | solution.py:184

commit v2 on v0

v2 whole, which is shorter than its diff:
```python
import functools

import jax
import jax.numpy as jnp
from jax import lax
from jax.experimental import pallas as pl
from jax.experimental.pallas import tpu as pltpu
from jax.sharding import PartitionSpec as P

MESH = pl.DeviceIdType.MESH
F32 = jnp.float32
BF16 = jnp.bfloat16
LANES = 128
CHUNKS = 8

OFFERED, FEATURES, AGGREGATE, NEIGH_BACK, SELF_BACK, RETURNED, SWAP, CHIPS, ROWS, PAIR = range(10)

INNER = (((1,), (0,)), ((), ()))
LAST = (((1,), (1,)), ((), ()))


def dot(a, b, dims=INNER):
    return lax.dot_general(a, b, dims, preferred_element_type=F32)


def split_dot(onehot, values):
    high = values.astype(BF16)
    low = (values - high.astype(F32)).astype(BF16)
    return dot(onehot, high) + dot(onehot, low)


def onehot(condition):
    return jnp.where(condition, 1.0, 0.0).astype(BF16)


def iota(shape, axis):
    return lax.broadcasted_iota(jnp.int32, shape, axis)


def layer_kernel(
    scale,
    feat_ref, adjacency_ref, dst_ref, peer_ref, slot_ref, offers_ref, labels_ref,
    w_self_ref, w_neigh_ref, w_class_ref,
    grad_ref, grad_self_ref, grad_neigh_ref, grad_class_ref,
    raw, tiles,
    offer_pad, pick_offer, put_offer, pick_source, put_source, pick_dest, put_dest, put_degree,
    to_nodes, to_columns,
    w_self_t, w_neigh_t, w_class_p, w_class_t,
    offered, incoming, feat_recv, agg_send, agg_recv, neigh_send, neigh_recv, self_send, self_recv,
    slot_send, slot_recv, weights, half, mine, got, sums, pair,
    gathered, products, degree, x_self, x_neigh,
    tile_sem, send, recv,
):
    row_count, col_count = lax.axis_size("row"), lax.axis_size("col")
    chip_count = col_count // 2
    row, col = lax.axis_index("row"), lax.axis_index("col")
    chip, core = col // 2, col % 2
    sibling = (row, chip * 2 + 1 - core)
    node_rows = col_count * 8
    tile_count = raw.shape[0]
    octs = tile_count // 8
    slot_rows = row_count * 16
    padded = incoming.shape[0] * 16

    def col_at(step):
        other = lax.rem(col + step, col_count)
        return other, (row, other)

    def row_at(step):
        other = lax.rem(row + step, row_count)
        return other, (other, col)

    def chip_at(step):
        other = lax.rem(chip + step, chip_count)
        return other, (row, other * 2 + core)

    def remote(source, target, phase, device):
        return pltpu.make_async_remote_copy(
            source, target, send.at[phase], recv.at[phase], device_id=device, device_id_type=MESH
        )

    def scatter(source, target, phase, count, at, here):
        @pl.loop(1, count)
        def _(step):
            other, device = at(step)
            remote(source.at[other], target.at[here], phase, device).start()

        target[here] = source[here]

    def wait_for(target, count, semaphore):
        others = target.at[pl.ds(0, count - 1)]
        pltpu.make_async_copy(others, others, semaphore).wait()

    barrier = pltpu.get_barrier_semaphore()

    @pl.loop(1, row_count)
    def _(step):
        pl.semaphore_signal(barrier, inc=1, device_id=row_at(step)[1], device_id_type=MESH)

    @pl.loop(1, col_count)
    def _(step):
        pl.semaphore_signal(barrier, inc=1, device_id=col_at(step)[1], device_id_type=MESH)

    per_chunk = tile_count // CHUNKS

    def chunk_copy(part):
        place = pl.ds(part * per_chunk, per_chunk)
        return pltpu.make_async_copy(adjacency_ref.at[0, place], raw.at[place], tile_sem.at[part])

    for part in range(CHUNKS):
        chunk_copy(part).start()

    offer_pad[...] = jnp.zeros_like(offer_pad)
    offer_pad[0:row_count, 0 : offers_ref.shape[2]] = offers_ref[0].astype(F32)
    offer_rows = dot(
        onehot(iota((padded, offer_pad.shape[0]), 0) // 16 == iota((padded, offer_pad.shape[0]), 1)),
        offer_pad[...].astype(BF16),
    )
    place = iota((padded, LANES), 0)
    offer_col = jnp.sum(
        jnp.where(place % 8 == iota((padded, LANES), 1), offer_rows, 0.0), axis=1, keepdims=True
    ).astype(jnp.int32)
    place_col = iota((padded, 1), 0)
    offer_col = (offer_col // 4) * 8 + offer_col % 4 + ((place_col // 8) % 2) * 4
    offer_col = jnp.where(place_col < slot_rows, offer_col, -1)
    pick = jnp.where(offer_col == iota((padded, node_rows), 1), 1.0, 0.0)
    pick_offer[...] = pick.astype(BF16)
    offered[...] = (
        dot(pick_offer[...], feat_ref[...].reshape(node_rows, LANES))
        .astype(BF16)
        .reshape(offered.shape)
    )
    incoming[row_count:] = jnp.zeros_like(incoming[row_count:])
    slot_recv[row_count:] = jnp.zeros_like(slot_recv[row_count:])

    pl.semaphore_wait(barrier, row_count + col_count - 2)
    scatter(offered, incoming, OFFERED, row_count, row_at, row)
    scatter(feat_ref, feat_recv, FEATURES, col_count, col_at, col)

    put_offer[...] = pick.T.astype(BF16)
    dst = dst_ref[...]
    source = peer_ref[...] * 16 + slot_ref[...]
    dst_row = (dst // 4) * 8 + dst % 4
    dst_rows = jnp.concatenate([dst_row, dst_row + 4], axis=1)
    source_rows = jnp.concatenate([source, source + 8], axis=1)
    pairs = dst_rows.shape[1]
    square = iota((pairs, pairs), 0) == iota((pairs, pairs), 1)

    def column(values):
        return jnp.sum(jnp.where(square, values, 0), axis=1, keepdims=True)

    put_dest[...] = onehot(iota((node_rows, pairs), 0) == dst_rows)
    pick_dest[...] = onehot(iota((pairs, node_rows), 1) == column(dst_rows))
    put_source[...] = onehot(iota((padded, pairs), 0) == source_rows)
    pick_source[...] = onehot(iota((pairs, padded), 1) == column(source_rows))
    block_of = iota((node_rows, tile_count), 0)
    put_degree[...] = onehot((block_of // 8) * 4 + block_of % 4 == dst)
    feat_count = col_count * 2
    one, two = iota((node_rows, node_rows), 0), iota((node_rows, node_rows), 1)
    to_nodes[...] = onehot(two == (one % feat_count) * 4 + one // feat_count)
    to_columns[...] = onehot(one == (two % feat_count) * 4 + two // feat_count)
    w_self_t[...] = w_self_ref[...].astype(F32).T.astype(BF16)
    w_neigh_t[...] = w_neigh_ref[...].astype(F32).T.astype(BF16)
    hidden_units, class_count = w_class_ref.shape
    class_rows = w_class_t.shape[0]
    w_class_p[...] = jnp.zeros_like(w_class_p)
    w_class_p[:, 0:class_count] = w_class_ref[...]
    w_class_t[...] = w_class_p[...].astype(F32).T.astype(BF16)[:class_rows]

    for part in range(CHUNKS):
        chunk_copy(part).wait()
        for oct_ in range(part * octs // CHUNKS, (part + 1) * octs // CHUNKS):
            for k in range(8):
                tiles[oct_, k // 2 * LANES : (k // 2 + 1) * LANES, k % 2 * LANES : (k % 2 + 1) * LANES] = (
                    raw[oct_ * 8 + k].astype(F32).astype(BF16)
                )

    wait_for(incoming, row_count, recv.at[OFFERED])
    gathered[...] = dot(pick_source[...], incoming[...].reshape(padded, LANES))
    kinds = iota((24, LANES), 0) % 8
    ones = jnp.ones((8, LANES), F32)
    for oct_ in range(octs):
        lines = jnp.concatenate(
            [gathered[8 * oct_ : 8 * oct_ + 8], gathered[tile_count + 8 * oct_ : tile_count + 8 * oct_ + 8], ones],
            axis=0,
        )
        left = jnp.concatenate(
            [jnp.where(kinds % 2 == half_, lines, 0.0) for half_ in range(2)], axis=1
        ).astype(BF16)
        out = dot(left, tiles[oct_], LAST)
        kept = out[:, 0:LANES]
        for quarter in range(1, 4):
            kept = jnp.where(
                kinds // 2 == quarter, out[:, quarter * LANES : (quarter + 1) * LANES], kept
            )
        for kind in range(3):
            at = kind * tile_count + 8 * oct_
            products[at : at + 8] = kept[8 * kind : 8 * kind + 8]
    divisor = jnp.maximum(split_dot(put_degree[...], products[pairs : pairs + tile_count]), 1.0)
    degree[...] = divisor
    agg_send[...] = (
        (split_dot(put_dest[...], products[0:pairs]) / divisor).astype(BF16).reshape(agg_send.shape)
    )
    scatter(agg_send, agg_recv, AGGREGATE, col_count, col_at, col)

    def node_columns(received, x_ref):
        moved = dot(to_nodes[...], received[...].reshape(node_rows, LANES)).astype(BF16)
        for block in range(4):
            x_ref[:, block * LANES : (block + 1) * LANES] = moved[
                block * feat_count : (block + 1) * feat_count
            ]

    wait_for(feat_recv, col_count, recv.at[FEATURES])
    node_columns(feat_recv, x_self)
    pre_self = dot(w_self_t[...], x_self[...])
    wait_for(agg_recv, col_count, recv.at[AGGREGATE])
    node_columns(agg_recv, x_neigh)

    pre = pre_self + dot(w_neigh_t[...], x_neigh[...])
    sigmoid = 1.0 / (1.0 + jnp.exp(-pre))
    hidden = (pre * sigmoid).astype(BF16)
    logits = dot(w_class_t[...], hidden)
    classes = iota(logits.shape, 0)
    exponent = jnp.where(classes < class_count, jnp.exp(logits), 0.0)
    soft = exponent / jnp.sum(exponent, axis=0, keepdims=True)
    label_row = jnp.concatenate([labels_ref[block : block + 1] for block in range(4)], axis=1)
    dlogits = (soft - jnp.where(classes == label_row, 1.0, 0.0)).astype(BF16)
    slope = sigmoid * (1.0 + pre * (1.0 - sigmoid))
    dpre = (dot(w_class_p[:, 0:class_rows], dlogits) * slope).astype(BF16)

    def block_rows(values):
        stacked = jnp.concatenate(
            [values[:, block * LANES : (block + 1) * LANES] for block in range(4)], axis=0
        )
        return dot(to_columns[...], stacked).astype(BF16).reshape(neigh_send.shape)

    my_degree = degree[pl.ds(pl.multiple_of(col * 8, 8), 8)]
    my_divisor = jnp.concatenate([my_degree[block : block + 1] for block in range(4)], axis=1)
    neigh_send[...] = block_rows((dot(w_neigh_ref[...], dpre) / my_divisor).astype(BF16))
    scatter(neigh_send, neigh_recv, NEIGH_BACK, col_count, col_at, col)
    self_send[...] = block_rows(dot(w_self_ref[...], dpre).astype(BF16))
    scatter(self_send, self_recv, SELF_BACK, col_count, col_at, col)

    both = jnp.concatenate([x_self[...], x_neigh[...]], axis=0)
    one, two = iota((2 * feat_count, 2 * feat_count), 0), iota((2 * feat_count, 2 * feat_count), 1)
    mixed = dot(
        onehot(two == (one // 8) * 4 + one % 4 + ((one // 4) % 2) * feat_count), both
    ).astype(BF16)
    weights[0] = (dot(mixed, dpre, LAST) * scale).reshape(half.shape)
    class_grad = dot(hidden, jnp.concatenate([dlogits, jnp.zeros((hidden_units - class_rows, dlogits.shape[1]), BF16)], axis=0), LAST)
    weights[1] = (class_grad * scale).reshape(half.shape)
    swap = remote(weights.at[1 - core], half, SWAP, sibling)
    swap.start()
    swap.wait()
    mine[...] = weights[core] + half[...]
    scatter(mine, got, CHIPS, chip_count, chip_at, chip)

    wait_for(neigh_recv, col_count, recv.at[NEIGH_BACK])
    gathered[...] = dot(pick_dest[...], neigh_recv[...].reshape(node_rows, LANES))
    kinds = iota((16, LANES), 0) % 8
    for oct_ in range(octs):
        lines = jnp.concatenate(
            [gathered[8 * oct_ : 8 * oct_ + 8], gathered[tile_count + 8 * oct_ : tile_count + 8 * oct_ + 8]],
            axis=0,
        )
        left = jnp.concatenate(
            [jnp.where(kinds // 2 == quarter, lines, 0.0) for quarter in range(4)], axis=1
        ).astype(BF16)
        out = dot(left, tiles[oct_])
        kept = jnp.where(kinds % 2 == 0, out[:, 0:LANES], out[:, LANES : 2 * LANES])
        for kind in range(2):
            at = kind * tile_count + 8 * oct_
            products[at : at + 8] = kept[8 * kind : 8 * kind + 8]
    slot_send[...] = split_dot(put_source[...], products[0:pairs]).reshape(slot_send.shape)
    scatter(slot_send, slot_recv, RETURNED, row_count, row_at, row)

    wait_for(got, chip_count, recv.at[CHIPS])
    sums[row] = jnp.sum(got[...], axis=0)

    @pl.loop(1, row_count)
    def _(step):
        remote(sums.at[row], sums.at[row], ROWS, row_at(step)[1]).start()

    wait_for(self_recv, col_count, recv.at[SELF_BACK])
    wait_for(slot_recv, row_count, recv.at[RETURNED])
    landed = split_dot(put_offer[...], slot_recv[...].reshape(padded, LANES))
    grad_ref[...] = (
        (self_recv[...].reshape(node_rows, LANES).astype(F32) + landed)
        .astype(BF16)
        .reshape(grad_ref.shape)
    )
    wait_for(sums, row_count, recv.at[ROWS])
    pair[core] = jnp.sum(sums[...], axis=0)
    last = remote(pair.at[core], pair.at[core], PAIR, sibling)
    last.start()
    last.wait()
    matrices, classes_part = pair[0], pair[1]
    first = core == 0
    grad_self_ref[...] = jnp.where(first, matrices[0:2], matrices[2:4])
    grad_neigh_ref[...] = jnp.where(first, matrices[4:6], matrices[6:8])
    grad_class_ref[...] = jnp.where(first, classes_part[0:4], classes_part[4:8])[:, 0:class_count]

    wait_for(incoming, row_count, send.at[OFFERED])
    for phase in (FEATURES, AGGREGATE, NEIGH_BACK, SELF_BACK):
        wait_for(feat_recv, col_count, send.at[phase])
    wait_for(slot_recv, row_count, send.at[RETURNED])
    wait_for(got, chip_count, send.at[CHIPS])
    wait_for(sums, row_count, send.at[ROWS])


def body(
    features_t, adjacency, tile_dst, tile_peer, tile_slot, offers, labels, w_self, w_neigh, w_class
):
    row_count = lax.axis_size("row")
    col_count = lax.axis_size("col")
    feat_cols, node_rows = features_t.shape
    tile_count = adjacency.shape[1]
    hidden_units, class_count = w_class.shape
    feats = feat_cols * col_count
    class_rows = -(-class_count // 16) * 16
    padded = -(-row_count // 8) * 8
    blocks = col_count * 8
    chips = col_count // 2
    rows_here = labels.shape[0]
    scale = (rows_here * row_count * col_count) ** (-0.5)
    by_col = (
        features_t.reshape(feat_cols, col_count, 4, LANES)
        .transpose(1, 0, 2, 3)
        .reshape(col_count, 8, LANES)
    )
    vmem = pl.BlockSpec(memory_space=pltpu.VMEM)
    message = pltpu.VMEM((col_count, 8, LANES), BF16)
    part = pltpu.VMEM((chips, 8, hidden_units), F32)
    grad, grad_self, grad_neigh, grad_class = pl.pallas_call(
        functools.partial(layer_kernel, scale),
        out_shape=(
            jax.ShapeDtypeStruct((col_count, 8, LANES), BF16),
            jax.ShapeDtypeStruct((feat_cols, hidden_units), F32),
            jax.ShapeDtypeStruct((feat_cols, hidden_units), F32),
            jax.ShapeDtypeStruct((hidden_units // col_count, class_count), F32),
        ),
        in_specs=[vmem, pl.BlockSpec(memory_space=pl.ANY)] + [vmem] * 8,
        out_specs=(vmem,) * 4,
        scratch_shapes=[
            pltpu.VMEM((tile_count, LANES, LANES), jnp.int32),
            pltpu.VMEM((tile_count // 8, 4 * LANES, 2 * LANES), BF16),
            pltpu.VMEM((padded, LANES), F32),
            pltpu.VMEM((padded * 16, blocks), BF16),
            pltpu.VMEM((blocks, padded * 16), BF16),
            pltpu.VMEM((2 * tile_count, padded * 16), BF16),
            pltpu.VMEM((padded * 16, 2 * tile_count), BF16),
            pltpu.VMEM((2 * tile_count, blocks), BF16),
            pltpu.VMEM((blocks, 2 * tile_count), BF16),
            pltpu.VMEM((blocks, tile_count), BF16),
            pltpu.VMEM((blocks, blocks), BF16),
            pltpu.VMEM((blocks, blocks), BF16),
            pltpu.VMEM((hidden_units, feats), BF16),
            pltpu.VMEM((hidden_units, feats), BF16),
            pltpu.VMEM((hidden_units, hidden_units), BF16),
            pltpu.VMEM((class_rows, hidden_units), BF16),
            pltpu.VMEM((padded, 16, LANES), BF16),
            pltpu.VMEM((padded, 16, LANES), BF16),
            message, message, message, message, message, message, message,
            pltpu.VMEM((padded, 16, LANES), F32),
            pltpu.VMEM((padded, 16, LANES), F32),
            pltpu.VMEM((2, chips, 8, hidden_units), F32),
            part, part, part,
            pltpu.VMEM((row_count, 8, hidden_units), F32),
            pltpu.VMEM((2, 8, hidden_units), F32),
            pltpu.VMEM((2 * tile_count, LANES), F32),
            pltpu.VMEM((3 * tile_count, LANES), F32),
            pltpu.VMEM((blocks, LANES), F32),
            pltpu.VMEM((feats, rows_here), BF16),
            pltpu.VMEM((feats, rows_here), BF16),
            pltpu.SemaphoreType.DMA((CHUNKS,)),
            pltpu.SemaphoreType.DMA((10,)),
            pltpu.SemaphoreType.DMA((10,)),
        ],
        compiler_params=pltpu.CompilerParams(
            collective_id=0, has_side_effects=True, vmem_limit_bytes=48 << 20
        ),
    )(
        by_col, adjacency, tile_dst, tile_peer, tile_slot, offers, labels.reshape(4, LANES),
        w_self, w_neigh, w_class,
    )
    grad_features = (
        grad.reshape(col_count, feat_cols, 4, LANES)
        .transpose(1, 0, 2, 3)
        .reshape(feat_cols, node_rows)
    )
    return grad_features, grad_self, grad_neigh, grad_class


def solution(mesh):
    in_specs = (
        P("col", "row"),
        P("row", None, None, None),
        P("row", None),
        P("row", None),
        P("row", None),
        P("row", None, None),
        P(("row", "col")),
        P(),
        P(),
        P(),
    )
    out_specs = (P("col", "row"), P("col", None), P("col", None), P("col", None))
    return jax.shard_map(body, mesh=mesh, in_specs=in_specs, out_specs=out_specs, check_vma=False)
```

time: 580 us -> 71.4 us (0.12)
  waiting for transfers between devices: 476 us -> 0 us
  Pallas kernels: 0 us -> 60.7 us
  starting transfers between devices: 50.8 us -> 0 us
  matrix products: 15.9 us -> 0 us
  between operations: 14.3 us -> 0.68 us
  other arithmetic: 11.6 us -> 0 us
    psum x1 -> x0, waiting for transfers between devices: 447 us -> none  [body(): lax.psum((self_part, neigh_part, class_part), ('row', 'col'))]
    pallas_call x0 -> x1, Pallas kernels: none -> 60.7 us  [body(): pl.pallas_call(functools.partial(layer_kernel, scale), out_shape=(jax.Sha...]
    all_to_all x6 -> x0, starting transfers between devices: 50.8 us -> none  [the longest x1 15.7 us: body(): lax.all_to_all(outgoing, 'row', split_axis=1, concat_axis=1, tiled=True)]
    all_to_all x6 -> x0, waiting for transfers between devices: 29.4 us -> none  [the longest x1 10.5 us: body(): lax.all_to_all(aggregate, 'col', split_axis=1, concat_axis=0, tiled=True)]
    dot_general x15 -> x0, matrix products: 15.9 us -> none  [the longest x1 5.68 us: body(): jnp.einsum('ftj,tij->fti', sources, tile_weights, preferred_element_type=...]
    unnamed x14 -> x17, local copies, waits for them, and re-layouts: 0.78 us -> 7.83 us
  transfers between devices with their start and end apart: 7 -> 0, of which waited for: 6 -> 0; matrix products, arithmetic and copies ran while one was open for 5% -> 0% of each run, Pallas kernels for 0% -> 0%
where the time goes in v2:
time: 71.4 us; the launch traced here: 71 us
  Pallas kernels  60.7 us (85%)
  local copies, waits for them, and re-layouts  9.63 us (13%)
    pallas_call x1, Pallas kernels, body(): pl.pallas_call(functools.partial(layer_kernel, scale), out_shape=(jax.Sha...  60.7 us
    unnamed x17, local copies, waits for them, and re-layouts  7.83 us

profile of v2, /device:TPU:1, one launch (start us, length us, event | category | flops | bytes accessed | tf_op | source)
XLA Modules:
  0.0 71.0 jit_solution(4923325535617236586)
XLA Ops:
  0.6 0.8 %copy.15.offers_ref = s32[1,12,8]{2,1,0:T(8,128)S(1)} copy(s32[1,12,8]{1,2,0:T(8,128)} %param.15) | data formatting | bytes 768 | tf_op args[5]
  1.4 1.0 %reshape.23 = bf16[2,64,4,128]{3,2,1,0:T(4,128)(2,1)S(1)} reshape(bf16[2,32768]{1,0:T(2,128)(2,1)} %param.10) | data formatting | bytes 262144 | tf_op jit(solution)/shard_map/reshape | solution.py:327
  2.5 1.0 %copy.16.w_class_ref = bf16[256,172]{1,0:T(8,128)(2,1)S(1)} copy(bf16[256,172]{0,1:T(8,128)(2,1)} %param.19) | data formatting | bytes 176128 | tf_op args[9]
  3.5 0.0 copy-start
  3.5 0.8 %copy-done = bf16[128,256]{1,0:T(8,128)(2,1)S(1)} copy-done((bf16[128,256]{1,0:T(8,128)(2,1)S(1)}, bf16[128,256]{1,0:T(8,128)(2,1)}, u32[]{:S(2)}) %copy-start) | copy-done | bytes 65560
  4.3 0.0 copy-start.1
  4.3 0.8 %copy-done.1 = bf16[128,256]{1,0:T(8,128)(2,1)S(1)} copy-done((bf16[128,256]{1,0:T(8,128)(2,1)S(1)}, bf16[128,256]{1,0:T(8,128)(2,1)}, u32[]{:S(2)}) %copy-start.1) | copy-done | bytes 65560
  5.2 0.0 copy-start.2
  5.2 0.7 copy-done.2
  5.8 0.0 copy-start.3
  5.8 0.7 copy-done.3
  6.5 0.0 copy-start.4
  6.5 0.7 copy-done.4
  7.1 0.0 copy-start.5
  7.1 0.7 copy-done.5
  7.8 60.7 %shard_map.129 = (bf16[64,8,128]{2,1,0:T(8,128)(2,1)S(1)}, f32[2,256]{1,0:T(2,128)S(1)}, f32[2,256]{1,0:T(2,128)S(1)}, f32[4,172]{1,0:T(4,128)S(1)}) custom-call(bf16[64,8,128]{2,1,0:T(8,128)(2,1)S(1)} %bitcast.7, s32[1,128,128,128]{3,2,1,0:T(8,128)} %adjacency_ref.1, s32[1,128]{1,0:T(1,128)S(1)} %copy-done.3, s32[1,128]{1,0:T(1,128)S(1)} %copy-done.4, ...), custom_call_target="tpu_custom_call" | custom-call | tf_op jit(solution)/shard_map/pallas_call | solution.py:334
  68.6 0.7 reshape.27
  69.2 0.6 copy.21
  69.8 0.6 copy.22
  70.4 0.6 copy.23
  (2 shorter events, 0.1 us)
Async XLA Ops:
  3.5 0.8 %copy-start = (bf16[128,256]{1,0:T(8,128)(2,1)S(1)}, bf16[128,256]{1,0:T(8,128)(2,1)}, u32[]{:S(2)}) copy-start(bf16[128,256]{1,0:T(8,128)(2,1)} %w_self_ref.1) | copy-start | bytes 196612
  4.3 0.8 %copy-start.1 = (bf16[128,256]{1,0:T(8,128)(2,1)S(1)}, bf16[128,256]{1,0:T(8,128)(2,1)}, u32[]{:S(2)}) copy-start(bf16[128,256]{1,0:T(8,128)(2,1)} %w_neigh_ref.1) | copy-start | bytes 196612
  5.2 0.7 copy-start.2
  5.8 0.7 copy-start.3
  6.5 0.7 copy-start.4
  7.1 0.7 copy-start.5

commit v3 on v2

v3 whole, which is shorter than its diff:
```python
import functools

import jax
import jax.numpy as jnp
from jax import lax
from jax.experimental import pallas as pl
from jax.experimental.pallas import tpu as pltpu
from jax.sharding import PartitionSpec as P

MESH = pl.DeviceIdType.MESH
F32 = jnp.float32
BF16 = jnp.bfloat16
LANES = 128
CHUNKS = 8

OFFERED, FEATURES, AGGREGATE, NEIGH_BACK, SELF_BACK, RETURNED, SWAP, CHIPS, ROWS = range(9)

INNER = (((1,), (0,)), ((), ()))
LAST = (((1,), (1,)), ((), ()))


def dot(a, b, dims=INNER):
    return lax.dot_general(a, b, dims, preferred_element_type=F32)


def split_dot(onehot, values):
    high = values.astype(BF16)
    low = (values - high.astype(F32)).astype(BF16)
    return dot(onehot, high) + dot(onehot, low)


def onehot(condition):
    return jnp.where(condition, 1.0, 0.0).astype(BF16)


def iota(shape, axis):
    return lax.broadcasted_iota(jnp.int32, shape, axis)


def layer_kernel(
    scale,
    feat_hbm, adjacency_ref, dst_hbm, peer_hbm, slot_hbm, offers_hbm, labels_hbm,
    w_self_hbm, w_neigh_hbm, w_class_hbm,
    grad_ref, grad_self_ref, grad_neigh_ref, grad_class_ref,
    feat_ref, dst_ref, peer_ref, slot_ref, offers_ref, labels_ref, w_self_ref, w_neigh_ref, w_class_ref,
    raw, tiles,
    offer_pad, pick_offer, put_offer, pick_source, put_source, pick_dest, put_dest, put_degree,
    to_nodes, to_columns, pick_rows,
    w_self_t, w_neigh_t, w_class_p, w_class_t,
    offered, incoming, feat_recv, agg_send, agg_recv, neigh_send, neigh_recv, self_send, self_recv,
    slot_send, slot_recv, weights, half, mine, got, sums,
    gathered, products, degree, x_self, x_neigh,
    tile_sem, input_sem, send, recv,
):
    row_count, col_count = lax.axis_size("row"), lax.axis_size("col")
    chip_count = col_count // 2
    row, col = lax.axis_index("row"), lax.axis_index("col")
    chip, core = col // 2, col % 2
    sibling = (row, chip * 2 + 1 - core)
    node_rows = col_count * 8
    tile_count = raw.shape[0]
    octs = tile_count // 8
    slot_rows = row_count * 16
    padded = incoming.shape[0] * 16

    def col_at(step):
        other = lax.rem(col + step, col_count)
        return other, (row, other)

    def row_at(step):
        other = lax.rem(row + step, row_count)
        return other, (other, col)

    def chip_at(step):
        other = lax.rem(chip + step, chip_count)
        return other, (row, other * 2 + core)

    def far_first(step, count):
        return count // 2 + (step // 2) * (2 * (step % 2) - 1)

    def remote(source, target, phase, device):
        return pltpu.make_async_remote_copy(
            source, target, send.at[phase], recv.at[phase], device_id=device, device_id_type=MESH
        )

    def scatter(source, target, phase, count, at, here):
        @pl.loop(1, count)
        def _(step):
            other, device = at(far_first(step, count))
            remote(source.at[other], target.at[here], phase, device).start()

        target[here] = source[here]

    def wait_for(target, count, semaphore):
        others = target.at[pl.ds(0, count - 1)]
        pltpu.make_async_copy(others, others, semaphore).wait()

    barrier = pltpu.get_barrier_semaphore()

    @pl.loop(1, row_count)
    def _(step):
        pl.semaphore_signal(barrier, inc=1, device_id=row_at(far_first(step, row_count))[1], device_id_type=MESH)

    @pl.loop(1, col_count)
    def _(step):
        pl.semaphore_signal(barrier, inc=1, device_id=col_at(far_first(step, col_count))[1], device_id_type=MESH)

    loads = [
        pltpu.make_async_copy(hbm, vmem, input_sem.at[number])
        for number, (hbm, vmem) in enumerate((
            (offers_hbm, offers_ref), (feat_hbm, feat_ref), (dst_hbm, dst_ref), (peer_hbm, peer_ref),
            (slot_hbm, slot_ref), (labels_hbm, labels_ref), (w_self_hbm, w_self_ref),
            (w_neigh_hbm, w_neigh_ref), (w_class_hbm, w_class_ref),
        ))
    ]
    for load in loads:
        load.start()

    per_chunk = tile_count // CHUNKS

    def chunk_copy(part):
        place = pl.ds(part * per_chunk, per_chunk)
        return pltpu.make_async_copy(adjacency_ref.at[0, place], raw.at[place], tile_sem.at[part])

    for part in range(CHUNKS):
        chunk_copy(part).start()

    offer_pad[...] = jnp.zeros_like(offer_pad)
    loads[0].wait()
    slots, peers = offers_ref.shape
    offer_pad[0:slots, 0:peers] = offers_ref[...].astype(F32)
    place = iota((padded, slots), 0)
    offer_rows = dot(
        onehot(place % slots == iota((padded, slots), 1)), offer_pad[...].astype(BF16)
    )
    place = iota((padded, LANES), 0)
    offer_col = jnp.sum(
        jnp.where(place // 16 == iota((padded, LANES), 1), offer_rows, 0.0), axis=1, keepdims=True
    ).astype(jnp.int32)
    place_col = iota((padded, 1), 0)
    offer_col = jnp.where(
        place_col < slot_rows, offer_col * 2 + (place_col // slots) % 2, -1
    )
    pick = jnp.where(offer_col == iota((padded, node_rows), 1), 1.0, 0.0)
    pick_offer[...] = pick.astype(BF16)
    loads[1].wait()
    offered[...] = (
        dot(pick_offer[...], feat_ref[...].reshape(node_rows, LANES))
        .astype(BF16)
        .reshape(offered.shape)
    )
    incoming[row_count:] = jnp.zeros_like(incoming[row_count:])
    slot_recv[row_count:] = jnp.zeros_like(slot_recv[row_count:])

    pl.semaphore_wait(barrier, row_count + col_count - 2)
    scatter(offered, incoming, OFFERED, row_count, row_at, row)
    scatter(feat_ref, feat_recv, FEATURES, col_count, col_at, col)

    put_offer[...] = pick.T.astype(BF16)
    for load in loads[2:]:
        load.wait()
    dst = dst_ref[...]
    source = peer_ref[...] * 16 + slot_ref[...]
    dst_rows = jnp.concatenate([dst * 2, dst * 2 + 1], axis=1)
    source_rows = jnp.concatenate([source, source + 8], axis=1)
    pairs = dst_rows.shape[1]
    square = iota((pairs, pairs), 0) == iota((pairs, pairs), 1)

    def column(values):
        return jnp.sum(jnp.where(square, values, 0), axis=1, keepdims=True)

    put_dest[...] = onehot(iota((node_rows, pairs), 0) == dst_rows)
    pick_dest[...] = onehot(iota((pairs, node_rows), 1) == column(dst_rows))
    put_source[...] = onehot(iota((padded, pairs), 0) == source_rows)
    pick_source[...] = onehot(iota((pairs, padded), 1) == column(source_rows))
    block_of = iota((node_rows, tile_count), 0)
    put_degree[...] = onehot(block_of // 2 == dst)
    feat_count = col_count * 2

    def received_row(place):
        feature = place % feat_count
        return (feature // 2) * 8 + (place // feat_count) * 2 + feature % 2

    one, two = iota((node_rows, 2 * feat_count), 0), iota((node_rows, 2 * feat_count), 1)
    owner = ((one % (4 * col_count)) // 8) * 2 + one // (4 * col_count)
    kind = one % 8
    pick_rows[0] = onehot(
        (kind < 4) & (two == owner * 2 + kind % 2 + (kind // 2) * feat_count)
    )
    pick_rows[1] = onehot((kind >= 4) & (two == owner * 4 + kind - 4))
    one, two = iota((node_rows, node_rows), 0), iota((node_rows, node_rows), 1)
    to_nodes[...] = onehot(two == received_row(one))
    to_columns[...] = onehot(one == received_row(two))
    w_self_t[...] = w_self_ref[...].astype(F32).T.astype(BF16)
    w_neigh_t[...] = w_neigh_ref[...].astype(F32).T.astype(BF16)
    class_count, hidden_units = w_class_ref.shape
    class_rows = w_class_t.shape[0]
    w_class_t[...] = jnp.zeros_like(w_class_t)
    w_class_t[0:class_count] = w_class_ref[...]
    w_class_p[...] = jnp.zeros_like(w_class_p)
    w_class_p[:, 0:class_rows] = w_class_t[...].astype(F32).T.astype(BF16)

    for part in range(CHUNKS):
        chunk_copy(part).wait()
        for oct_ in range(part * octs // CHUNKS, (part + 1) * octs // CHUNKS):
            for k in range(8):
                tiles[oct_, k // 2 * LANES : (k // 2 + 1) * LANES, k % 2 * LANES : (k % 2 + 1) * LANES] = (
                    raw[oct_ * 8 + k].astype(F32).astype(BF16)
                )

    def oct_products(lines, oct_):
        kinds = iota(lines.shape, 0) % 8
        left = jnp.concatenate(
            [jnp.where(kinds % 2 == half_, lines, 0.0) for half_ in range(2)], axis=1
        ).astype(BF16)
        out = dot(left, tiles[oct_], LAST)
        kept = out[:, 0:LANES]
        for quarter in range(1, 4):
            kept = jnp.where(
                kinds // 2 == quarter, out[:, quarter * LANES : (quarter + 1) * LANES], kept
            )
        return kept

    def tile_lines(oct_):
        return [
            gathered[kind * tile_count + 8 * oct_ : kind * tile_count + 8 * oct_ + 8]
            for kind in range(2)
        ]

    def keep(oct_, kept):
        for kind in range(2):
            at = kind * tile_count + 8 * oct_
            products[at : at + 8] = kept[8 * kind : 8 * kind + 8]

    ones = jnp.ones((8, LANES), F32)
    for oct_ in range(octs):
        products[8 * oct_ : 8 * oct_ + 8] = oct_products(ones, oct_)
    degree[...] = jnp.maximum(split_dot(put_degree[...], products[0:tile_count]), 1.0)

    wait_for(incoming, row_count, recv.at[OFFERED])
    gathered[...] = dot(pick_source[...], incoming[...].reshape(padded, LANES))
    for oct_ in range(octs):
        keep(oct_, oct_products(jnp.concatenate(tile_lines(oct_), axis=0), oct_))
    agg_send[...] = (
        (split_dot(put_dest[...], products[...]) / degree[...])
        .astype(BF16)
        .reshape(agg_send.shape)
    )
    scatter(agg_send, agg_recv, AGGREGATE, col_count, col_at, col)

    def node_columns(received, x_ref):
        moved = dot(to_nodes[...], received[...].reshape(node_rows, LANES)).astype(BF16)
        for block in range(4):
            x_ref[:, block * LANES : (block + 1) * LANES] = moved[
                block * feat_count : (block + 1) * feat_count
            ]

    wait_for(feat_recv, col_count, recv.at[FEATURES])
    node_columns(feat_recv, x_self)
    pre_self = dot(w_self_t[...], x_self[...])
    wait_for(agg_recv, col_count, recv.at[AGGREGATE])
    node_columns(agg_recv, x_neigh)

    pre = pre_self + dot(w_neigh_t[...], x_neigh[...])
    sigmoid = 1.0 / (1.0 + jnp.exp(-pre))
    hidden = (pre * sigmoid).astype(BF16)
    logits = dot(w_class_t[...], hidden)
    classes = iota(logits.shape, 0)
    exponent = jnp.where(classes < class_count, jnp.exp(logits), 0.0)
    soft = exponent / jnp.sum(exponent, axis=0, keepdims=True)
    label_row = jnp.concatenate([labels_ref[block : block + 1] for block in range(4)], axis=1)
    dlogits = (soft - jnp.where(classes == label_row, 1.0, 0.0)).astype(BF16)
    slope = sigmoid * (1.0 + pre * (1.0 - sigmoid))
    dpre = (dot(w_class_p[:, 0:class_rows], dlogits) * slope).astype(BF16)

    def block_rows(values):
        stacked = jnp.concatenate(
            [values[:, block * LANES : (block + 1) * LANES] for block in range(4)], axis=0
        )
        return dot(to_columns[...], stacked).astype(BF16).reshape(neigh_send.shape)

    my_degree = degree[pl.ds(pl.multiple_of(col * 8, 8), 8)]
    my_divisor = jnp.concatenate([my_degree[2 * block : 2 * block + 1] for block in range(4)], axis=1)
    both = jnp.concatenate([x_self[...], x_neigh[...]], axis=0)
    left = jnp.concatenate(
        [dot(pick_rows[0], both).astype(BF16), dot(pick_rows[1], hidden).astype(BF16)], axis=1
    )
    filler = jnp.zeros((hidden_units - class_rows, dlogits.shape[1]), BF16)
    right = jnp.concatenate([dpre, jnp.concatenate([dlogits, filler], axis=0)], axis=1)
    weights[...] = (dot(left, right, LAST) * scale).reshape(weights.shape)
    swap = remote(weights.at[1 - core], half, SWAP, sibling)
    swap.start()
    neigh_send[...] = block_rows((dot(w_neigh_ref[...], dpre) / my_divisor).astype(BF16))
    scatter(neigh_send, neigh_recv, NEIGH_BACK, col_count, col_at, col)
    swap.wait()
    mine[...] = (weights[core] + half[...]).astype(BF16)
    scatter(mine, got, CHIPS, chip_count, chip_at, chip)

    self_send[...] = block_rows(dot(w_self_ref[...], dpre).astype(BF16))
    scatter(self_send, self_recv, SELF_BACK, col_count, col_at, col)

    wait_for(neigh_recv, col_count, recv.at[NEIGH_BACK])
    gathered[...] = dot(pick_dest[...], neigh_recv[...].reshape(node_rows, LANES))
    kinds = iota((16, LANES), 0) % 8
    for oct_ in range(octs):
        lines = jnp.concatenate(tile_lines(oct_), axis=0)
        left = jnp.concatenate(
            [jnp.where(kinds // 2 == quarter, lines, 0.0) for quarter in range(4)], axis=1
        ).astype(BF16)
        out = dot(left, tiles[oct_])
        keep(oct_, jnp.where(kinds % 2 == 0, out[:, 0:LANES], out[:, LANES : 2 * LANES]))
    slot_send[...] = (
        split_dot(put_source[...], products[...]).astype(BF16).reshape(slot_send.shape)
    )
    scatter(slot_send, slot_recv, RETURNED, row_count, row_at, row)

    wait_for(got, chip_count, recv.at[CHIPS])
    sums[row] = jnp.sum(got[...].astype(F32), axis=0).astype(BF16)

    @pl.loop(1, row_count)
    def _(step):
        device = row_at(far_first(step, row_count))[1]
        remote(sums.at[row], sums.at[row], ROWS, device).start()

    wait_for(self_recv, col_count, recv.at[SELF_BACK])
    wait_for(slot_recv, row_count, recv.at[RETURNED])
    landed = dot(put_offer[...], slot_recv[...].reshape(padded, LANES))
    grad_ref[...] = (
        (self_recv[...].reshape(node_rows, LANES).astype(F32) + landed)
        .astype(BF16)
        .reshape(grad_ref.shape)
    )
    wait_for(sums, row_count, recv.at[ROWS])
    total = jnp.sum(sums[...].astype(F32), axis=0)
    grad_self_ref[...] = total[0:2]
    grad_neigh_ref[...] = total[2:4]
    grad_class_ref[...] = total[4:8, 0:class_count]

    wait_for(incoming, row_count, send.at[OFFERED])
    for phase in (FEATURES, AGGREGATE, NEIGH_BACK, SELF_BACK):
        wait_for(feat_recv, col_count, send.at[phase])
    wait_for(slot_recv, row_count, send.at[RETURNED])
    wait_for(got, chip_count, send.at[CHIPS])
    wait_for(sums, row_count, send.at[ROWS])


def finish_kernel(*refs):
    count = (len(refs) - 2) // 3
    inputs, outputs, staged = refs[:count], refs[count : 2 * count], refs[2 * count : 3 * count]
    arrived, left = refs[-2:]

    def copies(sources, targets, semaphore):
        return [
            pltpu.make_async_copy(sources[number], targets[number], semaphore.at[number])
            for number in range(count)
        ]

    reads, writes = copies(inputs, staged, arrived), copies(staged, outputs, left)
    for read in reads:
        read.start()
    for read, write in zip(reads, writes):
        read.wait()
        write.start()
    for write in writes:
        write.wait()


def body(
    features_t, adjacency, tile_dst, tile_peer, tile_slot, offers, labels, w_self, w_neigh, w_class
):
    row_count = lax.axis_size("row")
    col_count = lax.axis_size("col")
    feat_cols, node_rows = features_t.shape
    tile_count = adjacency.shape[1]
    hidden_units, class_count = w_class.shape
    feats = feat_cols * col_count
    class_rows = -(-class_count // 16) * 16
    padded = -(-row_count // 8) * 8
    blocks = col_count * 8
    chips = col_count // 2
    rows_here = labels.shape[0]
    scale = (rows_here * row_count * col_count) ** (-0.5)
    by_col = (
        features_t.reshape(feat_cols, col_count * 4, LANES)
        .transpose(1, 0, 2)
        .reshape(col_count, 8, LANES)
    )
    vmem = pl.BlockSpec(memory_space=pltpu.VMEM)
    message = pltpu.VMEM((col_count, 8, LANES), BF16)
    part = pltpu.VMEM((chips, 8, hidden_units), F32)
    grad, grad_self, grad_neigh, grad_class = pl.pallas_call(
        functools.partial(layer_kernel, scale),
        out_shape=(
            jax.ShapeDtypeStruct((col_count, 8, LANES), BF16),
            jax.ShapeDtypeStruct((feat_cols, hidden_units), F32),
            jax.ShapeDtypeStruct((feat_cols, hidden_units), F32),
            jax.ShapeDtypeStruct((hidden_units // col_count, class_count), F32),
        ),
        in_specs=[pl.BlockSpec(memory_space=pl.ANY)] * 10,
        out_specs=(vmem,) * 4,
        scratch_shapes=[
            message,
            pltpu.VMEM(tile_dst.shape, jnp.int32),
            pltpu.VMEM(tile_peer.shape, jnp.int32),
            pltpu.VMEM(tile_slot.shape, jnp.int32),
            pltpu.VMEM(offers.shape[:0:-1], jnp.int32),
            pltpu.VMEM((4, LANES), jnp.int32),
            pltpu.VMEM(w_self.shape, BF16),
            pltpu.VMEM(w_neigh.shape, BF16),
            pltpu.VMEM((class_count, hidden_units), BF16),
            pltpu.VMEM((tile_count, LANES, LANES), jnp.int32),
            pltpu.VMEM((tile_count // 8, 4 * LANES, 2 * LANES), BF16),
            pltpu.VMEM((8, LANES), F32),
            pltpu.VMEM((padded * 16, blocks), BF16),
            pltpu.VMEM((blocks, padded * 16), BF16),
            pltpu.VMEM((2 * tile_count, padded * 16), BF16),
            pltpu.VMEM((padded * 16, 2 * tile_count), BF16),
            pltpu.VMEM((2 * tile_count, blocks), BF16),
            pltpu.VMEM((blocks, 2 * tile_count), BF16),
            pltpu.VMEM((blocks, tile_count), BF16),
            pltpu.VMEM((blocks, blocks), BF16),
            pltpu.VMEM((blocks, blocks), BF16),
            pltpu.VMEM((2, blocks, 2 * feats), BF16),
            pltpu.VMEM((hidden_units, feats), BF16),
            pltpu.VMEM((hidden_units, feats), BF16),
            pltpu.VMEM((hidden_units, hidden_units), BF16),
            pltpu.VMEM((class_rows, hidden_units), BF16),
            pltpu.VMEM((padded, 16, LANES), BF16),
            pltpu.VMEM((padded, 16, LANES), BF16),
            message, message, message, message, message, message, message,
            pltpu.VMEM((padded, 16, LANES), BF16),
            pltpu.VMEM((padded, 16, LANES), BF16),
            pltpu.VMEM((2, chips, 8, hidden_units), F32),
            part,
            pltpu.VMEM((chips, 8, hidden_units), BF16),
            pltpu.VMEM((chips, 8, hidden_units), BF16),
            pltpu.VMEM((row_count, 8, hidden_units), BF16),
            pltpu.VMEM((2 * tile_count, LANES), F32),
            pltpu.VMEM((2 * tile_count, LANES), F32),
            pltpu.VMEM((blocks, LANES), F32),
            pltpu.VMEM((feats, rows_here), BF16),
            pltpu.VMEM((feats, rows_here), BF16),
            pltpu.SemaphoreType.DMA((CHUNKS,)),
            pltpu.SemaphoreType.DMA((9,)),
            pltpu.SemaphoreType.DMA((9,)),
            pltpu.SemaphoreType.DMA((9,)),
        ],
        compiler_params=pltpu.CompilerParams(
            collective_id=0, has_side_effects=True, vmem_limit_bytes=60 << 20
        ),
    )(
        by_col, adjacency, tile_dst, tile_peer, tile_slot, offers[0].T, labels.reshape(4, LANES),
        w_self, w_neigh, w_class.T,
    )
    anywhere = pl.BlockSpec(memory_space=pl.ANY)
    results = (grad, grad_self, grad_neigh, grad_class)
    grad, grad_self, grad_neigh, grad_class = pl.pallas_call(
        finish_kernel,
        out_shape=tuple(jax.ShapeDtypeStruct(result.shape, result.dtype) for result in results),
        in_specs=[anywhere] * 4,
        out_specs=(anywhere,) * 4,
        scratch_shapes=[pltpu.VMEM(result.shape, result.dtype) for result in results]
        + [pltpu.SemaphoreType.DMA((4,))] * 2,
        compiler_params=pltpu.CompilerParams(vmem_limit_bytes=60 << 20),
    )(*results)
    grad_features = (
        grad.reshape(col_count * 4, feat_cols, LANES)
        .transpose(1, 0, 2)
        .reshape(feat_cols, node_rows)
    )
    return grad_features, grad_self, grad_neigh, grad_class


def solution(mesh):
    in_specs = (
        P("col", "row"),
        P("row", None, None, None),
        P("row", None),
        P("row", None),
        P("row", None),
        P("row", None, None),
        P(("row", "col")),
        P(),
        P(),
        P(),
    )
    out_specs = (P("col", "row"), P("col", None), P("col", None), P("col", None))
    return jax.shard_map(body, mesh=mesh, in_specs=in_specs, out_specs=out_specs, check_vma=False)
```

time: 71.4 us -> 55.4 us (0.78)
  local copies, waits for them, and re-layouts: 9.63 us -> 0 us
  Pallas kernels: 60.7 us -> 54.6 us
    unnamed x17 -> x0, local copies, waits for them, and re-layouts: 7.83 us -> none
    pallas_call x1, Pallas kernels: 60.7 us -> 53 us  [body(): pl.pallas_call(functools.partial(layer_kernel, scale), out_shape=(jax.Sha...]
    reshape x3 -> x0, local copies, waits for them, and re-layouts: 1.75 us -> none  [the longest x2 1.06 us: body(): features_t.reshape(feat_cols, col_count, 4, LANES).transpose(1, 0, 2, 3)]
    pallas_call x0 -> x1, Pallas kernels: none -> 1.64 us  [body(): pl.pallas_call(finish_kernel, out_shape=tuple((jax.ShapeDtypeStruct(resul...]
where the time goes in v3:
time: 55.4 us; the launch traced here: 55.3 us
  Pallas kernels  54.6 us (99%)
  between operations  0.64 us (1%)
    pallas_call x1, Pallas kernels, body(): pl.pallas_call(functools.partial(layer_kernel, scale), out_shape=(jax.Sha...  53 us
    pallas_call x1, Pallas kernels, body(): pl.pallas_call(finish_kernel, out_shape=tuple((jax.ShapeDtypeStruct(resul...  1.64 us

profile of v3, /device:TPU:1, one launch (start us, length us, event | category | flops | bytes accessed | tf_op | source)
XLA Modules:
  0.0 55.3 jit_solution(16239650251723897665)
XLA Ops:
  0.6 53.0 %shard_map.129 = (bf16[64,8,128]{2,1,0:T(8,128)(2,1)}, f32[2,256]{1,0:T(2,128)}, f32[2,256]{1,0:T(2,128)}, f32[4,172]{1,0:T(4,128)}) custom-call(bf16[64,8,128]{2,1,0:T(8,128)(2,1)} %bitcast.15, s32[1,128,128,128]{3,2,1,0:T(8,128)} %adjacency_ref.1, s32[1,128]{1,0:T(1,128)} %dst_hbm.1, s32[1,128]{1,0:T(1,128)} %peer_hbm.1, s32[1,128]{1,0:T(1,128)} %slot_hbm.1, ...), custom_call_target="tpu_custom_call" | custom-call | tf_op jit(solution)/shard_map/pallas_call | solution.py:391
  53.6 1.6 %shard_map.130 = (bf16[64,8,128]{2,1,0:T(8,128)(2,1)}, f32[2,256]{1,0:T(2,128)}, f32[2,256]{1,0:T(2,128)}, f32[4,172]{1,0:T(4,128)}) custom-call(bf16[64,8,128]{2,1,0:T(8,128)(2,1)} %get-tuple-element.12.refs_0_, f32[2,256]{1,0:T(2,128)} %get-tuple-element.13.refs_1_, f32[2,256]{1,0:T(2,128)} %get-tuple-element.14.refs_2_, f32[4,172]{1,0:T(4,128)} %get-tuple-element.15.refs_3_), custom_call_target="tpu_custom_call" | custom-call | tf_op jit(solution)/shard_map/pallas_call | solution.py:457

commit v4 on v3

--- a/solution.py
+++ b/solution.py
@@ -49,7 +49,7 @@
     w_self_t, w_neigh_t, w_class_p, w_class_t,
     offered, incoming, feat_recv, agg_send, agg_recv, neigh_send, neigh_recv, self_send, self_recv,
     slot_send, slot_recv, weights, half, mine, got, sums,
-    gathered, products, degree, x_self, x_neigh,
+    gathered, products, degree, x_self, x_neigh, rows_self,
     tile_sem, input_sem, send, recv,
 ):
     row_count, col_count = lax.axis_size("row"), lax.axis_size("col")
@@ -258,6 +258,7 @@
     wait_for(feat_recv, col_count, recv.at[FEATURES])
     node_columns(feat_recv, x_self)
     pre_self = dot(w_self_t[...], x_self[...])
+    rows_self[...] = dot(pick_rows[0, :, 0:feat_count], x_self[...]).astype(BF16)
     wait_for(agg_recv, col_count, recv.at[AGGREGATE])
     node_columns(agg_recv, x_neigh)
 
@@ -281,22 +282,22 @@
 
     my_degree = degree[pl.ds(pl.multiple_of(col * 8, 8), 8)]
     my_divisor = jnp.concatenate([my_degree[2 * block : 2 * block + 1] for block in range(4)], axis=1)
-    both = jnp.concatenate([x_self[...], x_neigh[...]], axis=0)
-    left = jnp.concatenate(
-        [dot(pick_rows[0], both).astype(BF16), dot(pick_rows[1], hidden).astype(BF16)], axis=1
-    )
+    neigh_send[...] = block_rows((dot(w_neigh_ref[...], dpre) / my_divisor).astype(BF16))
+    scatter(neigh_send, neigh_recv, NEIGH_BACK, col_count, col_at, col)
+    rows_neigh = dot(pick_rows[0, :, feat_count : 2 * feat_count], x_neigh[...]).astype(BF16)
+    rows_class = dot(pick_rows[1], hidden).astype(BF16)
     filler = jnp.zeros((hidden_units - class_rows, dlogits.shape[1]), BF16)
-    right = jnp.concatenate([dpre, jnp.concatenate([dlogits, filler], axis=0)], axis=1)
-    weights[...] = (dot(left, right, LAST) * scale).reshape(weights.shape)
+    total = dot(rows_self[...] + rows_neigh, dpre, LAST) + dot(
+        rows_class, jnp.concatenate([dlogits, filler], axis=0), LAST
+    )
+    weights[...] = (total * scale).reshape(weights.shape)
     swap = remote(weights.at[1 - core], half, SWAP, sibling)
     swap.start()
-    neigh_send[...] = block_rows((dot(w_neigh_ref[...], dpre) / my_divisor).astype(BF16))
-    scatter(neigh_send, neigh_recv, NEIGH_BACK, col_count, col_at, col)
+    self_send[...] = block_rows(dot(w_self_ref[...], dpre).astype(BF16))
     swap.wait()
     mine[...] = (weights[core] + half[...]).astype(BF16)
     scatter(mine, got, CHIPS, chip_count, chip_at, chip)
 
-    self_send[...] = block_rows(dot(w_self_ref[...], dpre).astype(BF16))
     scatter(self_send, self_recv, SELF_BACK, col_count, col_at, col)
 
     wait_for(neigh_recv, col_count, recv.at[NEIGH_BACK])
@@ -440,6 +441,7 @@
             pltpu.VMEM((blocks, LANES), F32),
             pltpu.VMEM((feats, rows_here), BF16),
             pltpu.VMEM((feats, rows_here), BF16),
+            pltpu.VMEM((blocks, rows_here), BF16),
             pltpu.SemaphoreType.DMA((CHUNKS,)),
             pltpu.SemaphoreType.DMA((9,)),
             pltpu.SemaphoreType.DMA((9,)),

time: 55.4 us -> 54.6 us (0.986)
  Pallas kernels: 54.6 us -> 53.7 us
    pallas_call x1, Pallas kernels: 53 us -> 52 us  [body(): pl.pallas_call(functools.partial(layer_kernel, scale), out_shape=(jax.Sha...]
where the time goes in v4:
time: 54.6 us; the launch traced here: 54.3 us
  Pallas kernels  53.7 us (98%)
  between operations  0.64 us (1%)
    pallas_call x1, Pallas kernels, body(): pl.pallas_call(functools.partial(layer_kernel, scale), out_shape=(jax.Sha...  52 us
    pallas_call x1, Pallas kernels, body(): pl.pallas_call(finish_kernel, out_shape=tuple((jax.ShapeDtypeStruct(resul...  1.64 us

profile of v4, /device:TPU:1, one launch (start us, length us, event | category | flops | bytes accessed | tf_op | source)
XLA Modules:
  0.0 54.3 jit_solution(18046801059293919020)
XLA Ops:
  0.6 52.0 %shard_map.129 = (bf16[64,8,128]{2,1,0:T(8,128)(2,1)}, f32[2,256]{1,0:T(2,128)}, f32[2,256]{1,0:T(2,128)}, f32[4,172]{1,0:T(4,128)}) custom-call(bf16[64,8,128]{2,1,0:T(8,128)(2,1)} %bitcast.15, s32[1,128,128,128]{3,2,1,0:T(8,128)} %adjacency_ref.1, s32[1,128]{1,0:T(1,128)} %dst_hbm.1, s32[1,128]{1,0:T(1,128)} %peer_hbm.1, s32[1,128]{1,0:T(1,128)} %slot_hbm.1, ...), custom_call_target="tpu_custom_call" | custom-call | tf_op jit(solution)/shard_map/pallas_call | solution.py:392
  52.7 1.6 %shard_map.130 = (bf16[64,8,128]{2,1,0:T(8,128)(2,1)}, f32[2,256]{1,0:T(2,128)}, f32[2,256]{1,0:T(2,128)}, f32[4,172]{1,0:T(4,128)}) custom-call(bf16[64,8,128]{2,1,0:T(8,128)(2,1)} %get-tuple-element.12.refs_0_, f32[2,256]{1,0:T(2,128)} %get-tuple-element.13.refs_1_, f32[2,256]{1,0:T(2,128)} %get-tuple-element.14.refs_2_, f32[4,172]{1,0:T(4,128)} %get-tuple-element.15.refs_3_), custom_call_target="tpu_custom_call" | custom-call | tf_op jit(solution)/shard_map/pallas_call | solution.py:459
